TPU v7x, 256 devices: a whole 4x4x8 slice. The times are simulated.
256 devices in a mesh: seg: 16 (over y, z_hi, core), fft: 16 (over x, z_lo).
Axes of the slice: x: 4, y: 4, z: 8 (z_hi: 2, z_lo: 4; z = z_hi * 4 + z_lo), core: 2. Of those that a mesh axis runs over, the one named last changes fastest.
Arguments:
- baseband: bfloat16 [16, 16, 1, 2, 8, 61440], P('seg', 'fft'), may hold values from -6 to 6
- chirp_phase: float32 [16, 128, 16, 256], P('fft'), may hold values from -3.140625 to 3.140625
Outputs:
- filterbank: float32 [16, 15, 16, 128, 256], P('seg', None, 'fft')
All inputs are finite; a program needn't handle non-finite values.
Results may differ from a plain program's by a relative error of at most 0.0003.
Values may be sent and summed in bfloat16 or wider, within the bound.
A program may use at most 128 MiB of HBM per device.

v0:
```python
import math

import jax
import jax.numpy as jnp
from jax import lax
from jax.sharding import PartitionSpec as P

FFT_LEN = 8388608
CHANNELS = 256
SPLIT_E = 256
LOW = 128
SPLIT_H = 256


highest = lax.Precision.HIGHEST


def shifted(array, axis, by):
    size = lax.axis_size(axis)
    pairs = [(i, i + by) for i in range(size) if 0 <= i + by < size]
    return lax.ppermute(array, axis, pairs)


def rotor(indices, modulus, direction):
    radians = indices.astype(jnp.float32) * (direction * 2.0 * math.pi / modulus)
    return (jnp.cos(radians), jnp.sin(radians))


def wave_table(row_count, col_count, modulus, direction):
    row_index = lax.broadcasted_iota(jnp.int32, (row_count, col_count), 0)
    col_index = lax.broadcasted_iota(jnp.int32, (row_count, col_count), 1)
    return rotor(row_index * col_index % modulus, modulus, direction)


def contract_table(real_part, imag_part, contracted, cosine, sine_part, target):
    table_rank = len(contracted)
    from_real = jnp.moveaxis(
        jnp.stack([cosine, sine_part], axis=-1), (table_rank, table_rank + 1), (0, 1)
    )
    from_imag = jnp.moveaxis(
        jnp.stack([-sine_part, cosine], axis=-1), (table_rank, table_rank + 1), (0, 1)
    )
    table_dims = tuple(range(2, table_rank + 2))
    numbers = ((table_dims, contracted), ((), ()))
    joined = lax.dot_general(
        from_real, real_part, numbers, precision=highest, preferred_element_type=jnp.float32
    )
    joined = joined + lax.dot_general(
        from_imag, imag_part, numbers, precision=highest, preferred_element_type=jnp.float32
    )
    return (jnp.moveaxis(joined[:, 0], 0, target), jnp.moveaxis(joined[:, 1], 0, target))


def direct(real_part, imag_part, target, direction):
    length_k = real_part.shape[target]
    cosine, sine_part = wave_table(length_k, length_k, length_k, direction)
    return contract_table(real_part, imag_part, (target,), cosine, sine_part, target)


def spread(matrix, rank_total, target):
    return matrix.reshape((1,) * target + matrix.shape + (1,) * (rank_total - target - matrix.ndim))


def rotate(real_part, imag_part, cosine, sine_part):
    return (real_part * cosine - imag_part * sine_part, real_part * sine_part + imag_part * cosine)


def sectioned(real_part, imag_part, target, direction):
    length_k = real_part.shape[target]
    lower_len = 2 ** ((length_k.bit_length() - 1) // 2)
    upper_len = length_k // lower_len
    old_shape = real_part.shape
    two_digit = old_shape[:target] + (upper_len, lower_len) + old_shape[target + 1 :]
    real_part, imag_part = direct(
        real_part.reshape(two_digit), imag_part.reshape(two_digit), target, direction
    )
    cosine, sine_part = wave_table(upper_len, lower_len, length_k, direction)
    rank_total = len(two_digit)
    real_part, imag_part = rotate(
        real_part,
        imag_part,
        spread(cosine, rank_total, target),
        spread(sine_part, rank_total, target),
    )
    real_part, imag_part = direct(real_part, imag_part, target + 1, direction)
    real_part = jnp.swapaxes(real_part, target, target + 1).reshape(old_shape)
    imag_part = jnp.swapaxes(imag_part, target, target + 1).reshape(old_shape)
    return (real_part, imag_part)


def on_device(baseband, chirp_phase):
    lane_count = lax.axis_size("fft")
    member = lax.axis_index("fft")
    own_data = baseband[0, 0]
    pol_count = own_data.shape[0]
    inner_count = own_data.shape[2]
    own_columns = own_data.shape[3]
    tail_columns = own_columns // (lane_count - 1)
    column_len = SPLIT_E * SPLIT_H
    upper_count = SPLIT_E // lane_count
    block_rows = SPLIT_E // (lane_count * lane_count)
    received = shifted(own_data[:, :, :, :tail_columns], "seg", -1)
    first_cos, first_sin = wave_table(SPLIT_E, SPLIT_E, SPLIT_E, -1)
    samples = jnp.concatenate([own_data, received], axis=3)
    shaped = (pol_count, inner_count, samples.shape[3] // SPLIT_H, SPLIT_H)
    window_real = samples[:, 0].astype(jnp.float32).reshape(shaped)
    window_imag = samples[:, 1].astype(jnp.float32).reshape(shaped)
    real_part, imag_part = contract_table(window_real, window_imag, (2,), first_cos, first_sin, 2)
    cosine, sine_part = wave_table(SPLIT_E, SPLIT_H, column_len, -1)
    real_part, imag_part = rotate(
        real_part, imag_part, spread(cosine, 4, 2), spread(sine_part, 4, 2)
    )
    real_part, imag_part = direct(real_part, imag_part, 3, -1)
    grid_shape = (inner_count, SPLIT_E, SPLIT_H)
    residue = member + lane_count * lax.broadcasted_iota(jnp.int32, grid_shape, 0)
    frequency = lax.broadcasted_iota(jnp.int32, grid_shape, 1) + SPLIT_E * lax.broadcasted_iota(
        jnp.int32, grid_shape, 2
    )
    cosine, sine_part = rotor(residue * frequency % FFT_LEN, FFT_LEN, -1)
    real_part, imag_part = rotate(real_part, imag_part, cosine[None], sine_part[None])
    split_shape = (pol_count, inner_count, upper_count, lane_count, SPLIT_H)
    real_part = real_part.reshape(split_shape)
    imag_part = imag_part.reshape(split_shape)
    group_cos, group_sin = wave_table(LOW, LOW, LOW, -1)
    group_cos = group_cos.reshape(inner_count, lane_count, LOW)
    group_sin = group_sin.reshape(inner_count, lane_count, LOW)
    chirp_cos = jnp.cos(chirp_phase[0])
    chirp_sin = jnp.sin(chirp_phase[0])
    back_shape = (LOW, upper_count, SPLIT_H)
    residue = lax.broadcasted_iota(jnp.int32, back_shape, 0)
    frequency = (
        member
        + lane_count * lax.broadcasted_iota(jnp.int32, back_shape, 1)
        + SPLIT_E * lax.broadcasted_iota(jnp.int32, back_shape, 2)
    )
    undo_cos, undo_sin = rotor(residue * frequency % FFT_LEN, FFT_LEN, 1)
    exchanged = (
        lax.all_to_all(real_part, "fft", split_axis=3, concat_axis=3, tiled=True),
        lax.all_to_all(imag_part, "fft", split_axis=3, concat_axis=3, tiled=True),
    )
    part_real, part_imag = contract_table(
        exchanged[0], exchanged[1], (1, 3), group_cos, group_sin, 1
    )
    part_real, part_imag = rotate(part_real, part_imag, chirp_cos, chirp_sin)
    part_real, part_imag = direct(part_real, part_imag, 1, 1)
    real_part, imag_part = rotate(part_real, part_imag, undo_cos, undo_sin)
    by_lane = (pol_count, inner_count, lane_count, upper_count, SPLIT_H)
    exchanged = (
        lax.all_to_all(real_part.reshape(by_lane), "fft", split_axis=2, concat_axis=2, tiled=True),
        lax.all_to_all(imag_part.reshape(by_lane), "fft", split_axis=2, concat_axis=2, tiled=True),
    )
    part_real = jnp.swapaxes(exchanged[0], 2, 3).reshape(-1, inner_count, SPLIT_E, SPLIT_H)
    part_imag = jnp.swapaxes(exchanged[1], 2, 3).reshape(-1, inner_count, SPLIT_E, SPLIT_H)
    part_real, part_imag = sectioned(part_real, part_imag, 3, 1)
    turn_cos, turn_sin = wave_table(SPLIT_E, SPLIT_H, column_len, 1)
    part_real, part_imag = rotate(
        part_real, part_imag, spread(turn_cos, 4, 2), spread(turn_sin, 4, 2)
    )
    real_part, imag_part = sectioned(part_real, part_imag, 2, 1)
    by_block = (pol_count, inner_count, lane_count, lane_count, block_rows, SPLIT_H)
    real_part, imag_part = (
        lax.all_to_all(real_part.reshape(by_block), "fft", split_axis=3, concat_axis=3, tiled=True),
        lax.all_to_all(imag_part.reshape(by_block), "fft", split_axis=3, concat_axis=3, tiled=True),
    )
    permutation = (0, 1, 3, 2, 4, 5)
    final_shape = (pol_count, LOW, lane_count, block_rows, SPLIT_H)
    real_part = jnp.transpose(real_part, permutation).reshape(final_shape)
    imag_part = jnp.transpose(imag_part, permutation).reshape(final_shape)
    normalizer = 1.0 / FFT_LEN
    kept_real = real_part[:, :, : lane_count - 1] * normalizer
    kept_imag = imag_part[:, :, : lane_count - 1] * normalizer
    even_real = kept_real[..., 0::2]
    even_imag = kept_imag[..., 0::2]
    odd_real = kept_real[..., 1::2]
    odd_imag = kept_imag[..., 1::2]
    turn_cos, turn_sin = rotor(lax.iota(jnp.int32, LOW), CHANNELS, -1)
    minus_real, minus_imag = rotate(
        even_real - odd_real, even_imag - odd_imag, spread(turn_cos, 5, 1), spread(turn_sin, 5, 1)
    )
    filter_cos, filter_sin = wave_table(LOW, LOW, LOW, -1)

    def detect(part_real, part_imag):
        spectral_real, spectral_imag = contract_table(
            part_real, part_imag, (1,), filter_cos, filter_sin, 4
        )
        return (
            jnp.sum(spectral_real * spectral_real + spectral_imag * spectral_imag, axis=0)
            / CHANNELS
        )

    power_even = detect(even_real + odd_real, even_imag + odd_imag)
    power_odd = detect(minus_real, minus_imag)
    detected = jnp.stack([power_even, power_odd], axis=-1).reshape(lane_count - 1, -1, CHANNELS)
    return detected[None, :, None]


def solution(mesh):
    placed = (P("seg", "fft", None, None, None, None), P("fft", None, None, None))
    return jax.shard_map(
        on_device,
        mesh=mesh,
        in_specs=placed,
        out_specs=P("seg", None, "fft", None, None),
        check_vma=False,
    )
```

profile of v0, /device:TPU:26, one launch (start us, length us, event | category | flops | bytes accessed | tf_op | source)
XLA Modules:
  0.0 653.5 jit_solution(2232532702474801775)
XLA Ops:
  0.9 8.7 %collective-permute-start = (bf16[1,2,8,4096]{3,2,1,0:T(8,128)(2,1)S(1)}, bf16[1,2,8,4096]{3,2,1,0:T(8,128)(2,1)S(1)}, u32[]{:S(2)}, u32[]{:S(2)}) collective-permute-start(bf16[1,2,8,4096]{3,2,1,0:T(8,128)(2,1)S(1)} %slice.116), channel_id=1, source_target_pairs={{16,0},{32,16},{48,32},{64,48},{80,64},{96,80},{112,96},{128,112},... | collective-permute-start | bytes 393224 | tf_op jit(solution)/shard_map/ppermute | solution.py:21
  25.7 10.1 %multiply_add_fusion.2 = (f32[1,8,256,256]{3,2,1,0:T(8,128)}, f32[1,8,256,256]{3,2,1,0:T(8,128)S(1)}) fusion(f32[256,2,1,8,256]{0,4,3,2,1:T(8,128)S(1)} %bitcast.352, f32[256,2,1,8,256]{0,4,3,1,2:T(8,128)S(1)} %bitcast.353, s32[256]{0:T(256)S(1)} %iota_multiply_fusion, s32[8]{0:T(128)S(1)} %multiply_add_fusion.6), kind=kLoop, calls=%fused_computation.81 | loop fusion | flops 11010048 | bytes 8389664 | tf_op jit(solution)/shard_map/add | solution.py:65
  49.0 45.3 %all-to-all-done = f32[1,8,16,16,256]{4,1,2,0,3:T(8,128)S(1)} async-done(((f32[1,8,16,16,256]{4,1,2,0,3:T(8,128)}), f32[1,8,16,16,256]{4,1,2,0,3:T(8,128)S(1)}, u32[]{:S(2)}, u32[]{:S(2)}) %all-to-all-start) | async-done | bytes 2097184 | tf_op jit(solution)/shard_map/all_to_all | solution.py:138
  94.3 10.7 %all-to-all-start.1 = ((f32[1,8,16,16,256]{4,1,2,0,3:T(8,128)}), f32[1,8,16,16,256]{4,1,2,0,3:T(8,128)}, u32[]{:S(2)}, u32[]{:S(2)}) async-start(f32[1,8,16,16,256]{4,1,2,0,3:T(8,128)} %copy.83), calls=%async_computation.1 | async-start | bytes 4194304 | tf_op jit(solution)/shard_map/all_to_all | solution.py:139
  111.9 41.0 %all-to-all-done.1 = f32[1,8,16,16,256]{4,1,2,0,3:T(8,128)} async-done(((f32[1,8,16,16,256]{4,1,2,0,3:T(8,128)}), f32[1,8,16,16,256]{4,1,2,0,3:T(8,128)}, u32[]{:S(2)}, u32[]{:S(2)}) %all-to-all-start.1) | async-done | bytes 2097184 | tf_op jit(solution)/shard_map/all_to_all | solution.py:139
  153.0 8.7 %bitcast_add_fusion = f32[128,2,16,256]{3,0,2,1:T(8,128)S(1)} fusion(f32[128,2,16,256,1]{3,0,4,2,1:T(8,128)} %fusion.25, f32[1,8,16,16,256]{4,1,2,0,3:T(8,128)} %all-to-all-done.1, f32[8,16,128,1]{2,1,0,3:T(8,128)S(1)} %get-tuple-element.31, f32[8,16,128,1]{2,1,0,3:T(8,128)S(1)} %get-tuple-element.29), kind=kOutput, calls=%fused_computation | convolution fusion | flops 1611694080 | bytes 10616832 | tf_op jit(solution)/shard_map/dot_general | solution.py:48
  161.7 11.4 %fusion.22 = f32[128,2,16,256]{3,0,2,1:T(8,128)S(1)} fusion(f32[128,2,1,16,256]{4,0,3,2,1:T(8,128)S(1)} %bitcast.344, f32[128,2,1,16,256]{4,0,3,1,2:T(8,128)S(1)} %bitcast.345, f32[1,128,16,256]{3,2,1,0:T(8,128)S(1)} %copy-done.1, f32[128,128,1]{0,1,2:T(8,128)S(1)} %get-tuple-element.36, f32[128,128,1]{0,1,2:T(8,128)S(1)} %get-tuple-element.37), kind=kOutput, calls=%fused_computation.54 | convolution fusion | flops 1612218368 | bytes 10616832 | tf_op jit(solution)/shard_map/dot_general | solution.py:45
  173.1 11.7 %add_bitcast_fusion.2 = f32[128,2,1,16,256]{4,0,3,1,2:T(8,128)S(1)} fusion(f32[128,2,16,256]{3,0,2,1:T(8,128)S(1)} %fusion.22, f32[128,2,1,16,256]{4,0,3,2,1:T(8,128)S(1)} %bitcast.346, f32[128,2,1,16,256]{4,0,3,1,2:T(8,128)S(1)} %bitcast.347, f32[1,128,16,256]{3,2,1,0:T(8,128)S(1)} %copy-done.1, f32[128,128,1]{0,1,2:T(8,128)S(1)} %get-tuple-element.37, ...), kind=kOutput, calls=%fused_computation.3 | convolution fusion | flops 1613266944 | bytes 14811136 | tf_op jit(solution)/shard_map/dot_general | solution.py:48
  185.2 11.5 %multiply_add_fusion.1 = (f32[1,8,16,16,256]{4,3,1,0,2:T(8,128)}, f32[1,8,16,16,256]{4,3,1,0,2:T(8,128)S(1)}) fusion(f32[1,8,16,16,256]{4,2,1,3,0:T(8,128)S(1)} %bitcast.362, f32[1,8,16,16,256]{4,2,1,3,0:T(8,128)S(1)} %bitcast.361, s32[256]{0:T(256)S(1)} %iota_multiply_fusion, s32[16]{0:T(128)S(1)} %multiply_add_fusion.5), kind=kLoop, calls=%fused_computation.73 | loop fusion | flops 12058624 | bytes 8389696 | tf_op jit(solution)/shard_map/add | solution.py:65
  196.7 54.0 %all_to_all.30 = f32[1,8,16,16,256]{4,3,1,0,2:T(8,128)} all-to-all(f32[1,8,16,16,256]{4,3,1,0,2:T(8,128)S(1)} %get-tuple-element.14), channel_id=1, replica_groups=mesh['seg'=16,'fft'=16] {'fft'}, dimensions={2} | all-to-all | bytes 4194304 | tf_op jit(solution)/shard_map/all_to_all | solution.py:149
  261.6 8.7 %reshape.807 = f32[8,256,16,16]{3,2,1,0:T(8,128)} reshape(f32[1,8,16,16,256]{4,3,2,1,0:T(8,128)S(1)} %copy.90) | data formatting | bytes 4194304 | tf_op jit(solution)/shard_map/reshape.22
  270.3 12.0 %copy.91 = f32[8,256,16,16]{1,2,3,0:T(8,128)S(1)} copy(f32[8,256,16,16]{3,2,1,0:T(8,128)} %reshape.807) | data formatting | bytes 4194304 | tf_op jit(solution)/shard_map/reshape.22
  282.3 22.2 %all-to-all-done.3 = f32[1,8,16,16,256]{4,3,1,0,2:T(8,128)} async-done(((f32[1,8,16,16,256]{4,3,1,0,2:T(8,128)}), f32[1,8,16,16,256]{4,3,1,0,2:T(8,128)}, u32[]{:S(2)}, u32[]{:S(2)}) %all-to-all-start.3) | async-done | bytes 2097184 | tf_op jit(solution)/shard_map/all_to_all | solution.py:150
  308.6 10.5 %reshape.808 = f32[8,256,16,16]{3,2,1,0:T(8,128)} reshape(f32[1,8,16,16,256]{4,3,2,1,0:T(8,128)} %copy.94) | data formatting | bytes 4194304 | tf_op jit(solution)/shard_map/reshape.47
  319.1 13.3 %copy.95 = f32[8,256,16,16]{1,2,3,0:T(8,128)} copy(f32[8,256,16,16]{3,2,1,0:T(8,128)} %reshape.808) | data formatting | bytes 4194304 | tf_op jit(solution)/shard_map/reshape.47
  351.2 11.4 %copy.99 = f32[1,8,256,16,16]{4,3,2,1,0:T(8,128)} copy(f32[1,8,256,16,16]{2,3,4,1,0:T(8,128)S(1)} %get-tuple-element.19) | data formatting | bytes 4194304 | tf_op jit(solution)/shard_map/transpose;transpose | solution.py:86
  362.6 11.4 %reshape.811 = f32[8,16,16,256]{3,2,1,0:T(8,128)S(1)} reshape(f32[1,8,256,16,16]{4,3,2,1,0:T(8,128)} %copy.99) | data formatting | bytes 4194304 | tf_op jit(solution)/shard_map/reshape | solution.py:86
  374.0 12.3 %copy.100 = f32[1,8,256,16,16]{4,3,2,1,0:T(8,128)} copy(f32[1,8,256,16,16]{2,3,4,1,0:T(8,128)} %get-tuple-element.20) | data formatting | bytes 4194304 | tf_op jit(solution)/shard_map/transpose;transpose | solution.py:87
  386.2 12.9 %reshape.812 = f32[8,16,16,256]{3,2,1,0:T(8,128)} reshape(f32[1,8,256,16,16]{4,3,2,1,0:T(8,128)} %copy.100) | data formatting | bytes 4194304 | tf_op jit(solution)/shard_map/reshape | solution.py:87
  433.0 44.8 %all-to-all-done.4 = f32[1,8,16,16,1,256]{5,2,1,4,0,3:T(8,128)S(1)} async-done(((f32[1,8,16,16,1,256]{5,2,1,4,0,3:T(8,128)}), f32[1,8,16,16,1,256]{5,2,1,4,0,3:T(8,128)S(1)}, u32[]{:S(2)}, u32[]{:S(2)}) %all-to-all-start.4) | async-done | bytes 2097184 | tf_op jit(solution)/shard_map/all_to_all | solution.py:162
  486.0 37.5 %slice.106 = f32[1,128,15,1,128]{4,2,1,3,0:T(8,128)S(1)} slice(f32[1,128,15,1,256]{4,2,1,3,0:T(8,128)S(1)} %slice_multiply_fusion.1), slice={[0:1:1], [0:128:1], [0:15:1], [0:1:1], [0:256:2]} | slice | bytes 1966080 | tf_op jit(solution)/shard_map/slice | solution.py:172
  523.5 37.9 %slice.107 = f32[1,128,15,1,128]{4,2,1,3,0:T(8,128)} slice(f32[1,128,15,1,256]{4,2,1,3,0:T(8,128)S(1)} %slice_multiply_fusion.1), slice={[0:1:1], [0:128:1], [0:15:1], [0:1:1], [1:256:2]} | slice | bytes 1966080 | tf_op jit(solution)/shard_map/slice | solution.py:174
  563.4 37.9 %slice.110 = f32[1,128,15,1,128]{4,2,1,3,0:T(8,128)} slice(f32[1,128,15,1,256]{4,2,1,3,0:T(8,128)S(1)} %slice_multiply_fusion), slice={[0:1:1], [0:128:1], [0:15:1], [0:1:1], [0:256:2]} | slice | bytes 1966080 | tf_op jit(solution)/shard_map/slice | solution.py:173
  601.3 38.1 %slice.111 = f32[1,128,15,1,128]{4,2,1,3,0:T(8,128)} slice(f32[1,128,15,1,256]{4,2,1,3,0:T(8,128)S(1)} %slice_multiply_fusion), slice={[0:1:1], [0:128:1], [0:15:1], [0:1:1], [1:256:2]} | slice | bytes 1966080 | tf_op jit(solution)/shard_map/slice | solution.py:175
  (69 shorter events, 128.8 us)
Async XLA Ops:
  0.9 11.8 %collective-permute-start = (bf16[1,2,8,4096]{3,2,1,0:T(8,128)(2,1)S(1)}, bf16[1,2,8,4096]{3,2,1,0:T(8,128)(2,1)S(1)}, u32[]{:S(2)}, u32[]{:S(2)}) collective-permute-start(bf16[1,2,8,4096]{3,2,1,0:T(8,128)(2,1)S(1)} %slice.116), channel_id=1, source_target_pairs={{16,0},{32,16},{48,32},{64,48},{80,64},{96,80},{112,96},{128,112},... | collective-permute-start | bytes 393224 | tf_op jit(solution)/shard_map/ppermute | solution.py:21
  38.3 56.0 %all-to-all-start = ((f32[1,8,16,16,256]{4,1,2,0,3:T(8,128)}), f32[1,8,16,16,256]{4,1,2,0,3:T(8,128)S(1)}, u32[]{:S(2)}, u32[]{:S(2)}) async-start(f32[1,8,16,16,256]{4,1,2,0,3:T(8,128)} %copy.81), calls=%async_computation | async-start | bytes 4194304 | tf_op jit(solution)/shard_map/all_to_all | solution.py:138
  94.3 58.7 %all-to-all-start.1 = ((f32[1,8,16,16,256]{4,1,2,0,3:T(8,128)}), f32[1,8,16,16,256]{4,1,2,0,3:T(8,128)}, u32[]{:S(2)}, u32[]{:S(2)}) async-start(f32[1,8,16,16,256]{4,1,2,0,3:T(8,128)} %copy.83), calls=%async_computation.1 | async-start | bytes 4194304 | tf_op jit(solution)/shard_map/all_to_all | solution.py:139
  153.0 8.7 %copy-start.1 = (f32[1,128,16,256]{3,2,1,0:T(8,128)S(1)}, f32[1,128,16,256]{3,2,1,0:T(8,128)}, u32[]{:S(2)}) copy-start(f32[1,128,16,256]{3,2,1,0:T(8,128)} %param.3) | copy-start | bytes 6291460
  250.6 53.9 %all-to-all-start.3 = ((f32[1,8,16,16,256]{4,3,1,0,2:T(8,128)}), f32[1,8,16,16,256]{4,3,1,0,2:T(8,128)}, u32[]{:S(2)}, u32[]{:S(2)}) async-start(f32[1,8,16,16,256]{4,3,1,0,2:T(8,128)} %get-tuple-element.13), calls=%async_computation.3 | async-start | bytes 4194304 | tf_op jit(solution)/shard_map/all_to_all | solution.py:150
  332.4 3.5 copy-start
  423.5 54.3 %all-to-all-start.4 = ((f32[1,8,16,16,1,256]{5,2,1,4,0,3:T(8,128)}), f32[1,8,16,16,1,256]{5,2,1,4,0,3:T(8,128)S(1)}, u32[]{:S(2)}, u32[]{:S(2)}) async-start(f32[1,8,16,16,1,256]{5,2,1,4,0,3:T(8,128)} %copy.106), calls=%async_computation.4 | async-start | bytes 4194304 | tf_op jit(solution)/shard_map/all_to_all | solution.py:162
  477.8 83.6 %all-to-all-start.5 = ((f32[1,8,16,16,1,256]{5,2,1,4,0,3:T(8,128)}), f32[1,8,16,16,1,256]{5,2,1,4,0,3:T(8,128)}, u32[]{:S(2)}, u32[]{:S(2)}) async-start(f32[1,8,16,16,1,256]{5,2,1,4,0,3:T(8,128)} %copy.109), calls=%async_computation.5 | async-start | bytes 4194304 | tf_op jit(solution)/shard_map/all_to_all | solution.py:163
where the time goes:
time: 663 us; the launch traced here: 653 us
  local copies, waits for them, and re-layouts  273 us (41%)
  waiting for transfers between devices  153 us (23%)
  matrix products  90.1 us (14%)
  blocking collectives  54 us (8%)
  starting transfers between devices  46.4 us (7%)
  other arithmetic  36 us (5%)
    all_to_all x1, blocking collectives, on_device(): lax.all_to_all(real_part.reshape(by_lane), 'fft', split_axis=2, concat_ax...  54 us
    dot_general x10, matrix products, contract_table(): lax.dot_general(from_imag, imag_part, numbers, precision=highest, preferr...  46.8 us
    all_to_all x1, waiting for transfers between devices, on_device(): lax.all_to_all(real_part, 'fft', split_axis=3, concat_axis=3, tiled=True)  45.3 us
    all_to_all x1, waiting for transfers between devices, on_device(): lax.all_to_all(real_part.reshape(by_block), 'fft', split_axis=3, concat_a...  44.8 us
    another operation x4, local copies, waits for them, and re-layouts  44.5 us
    dot_general x10, matrix products, contract_table(): lax.dot_general(from_real, real_part, numbers, precision=highest, preferr...  43.3 us
    all_to_all x1, waiting for transfers between devices, on_device(): lax.all_to_all(imag_part, 'fft', split_axis=3, concat_axis=3, tiled=True)  41 us
    slice x1, local copies, waits for them, and re-layouts, on_device(): odd_imag = kept_imag[..., 1::2]  38.1 us
  transfers between devices with their start and end apart: 6, of which 4 were waited for; matrix products, arithmetic and copies ran while one was open for 18% of the time, Pallas kernels for 0%

commit v1 on v0

v1 whole, which is shorter than its diff:
```python
import functools

import jax
import jax.numpy as jnp
import ml_dtypes
import numpy as np
from jax import lax
from jax.experimental import pallas as pl
from jax.experimental.pallas import tpu as pltpu
from jax.sharding import PartitionSpec as P

FFT_LEN = 8388608
LANES = 16
SEGS = 16
OWN = 61440
TAIL = 4096
COLS = OWN + TAIL
JC = 4
NC = 16 // JC
QC = 4
RQ = 32
KNEE = 4.0
POWER = 20
SHIFT = 2.0**-6.25
TINY = 1e-36

MESH = pl.DeviceIdType.MESH
f32 = jnp.float32
bf16 = jnp.bfloat16


def unit(numerator, modulus, direction):
    angle = (np.asarray(numerator, np.int64) % modulus) * (direction * 2.0 * np.pi / modulus)
    return np.cos(angle), np.sin(angle)


def halves(table):
    table = table.astype(np.float32)
    high = table.astype(ml_dtypes.bfloat16)
    low = (table - high.astype(np.float32)).astype(ml_dtypes.bfloat16)
    return high, low


@functools.lru_cache(maxsize=None)
def tables():
    n = FFT_LEN
    r16, r128, r256 = np.arange(16), np.arange(128), np.arange(256)
    out = {}
    c, s = unit(
        r16[None, :, None] * r16[None, None, :] * (n // 256) + r16[:, None, None] * r16[None, None, :],
        n,
        -1,
    )
    out["s1"] = np.stack([c, s]).astype(np.float32).reshape(2, -1)
    c, s = unit(r16[:, None] * r16[None, :], 256, 1)
    out["s2"] = np.stack([c, s]).astype(np.float32).reshape(2, -1)
    e = r16[:, None] + 16 * r16[None, :]
    ib = 16 * np.arange(8)[:, None] + 128 * r256[None, :]
    c, s = unit(e[:, :, None, None] * ib[None, None], n, -1)
    out["pw"] = np.stack([c, s]).astype(np.float32)
    c, s = unit(r256[:, None] * r256[None, :], 256, -1)
    out["g"] = halves(np.block([[c, s], [-s, c]]))
    res = r16[:, None] + 16 * np.arange(8)[None, :]
    c, s = unit(res[:, :, None] * r256[None, None, :], 32768, -1)
    out["c2"] = np.stack([c, s], axis=1).astype(np.float32)
    src, i = r16[:, None], np.arange(8)[None, :]
    num = (src + 16 * i)[None, None] * r128[None, :, None, None] * (n // 128)
    num = num + src[None, None] * 16 * r16[:, None, None, None]
    c, s = unit(num, n, -1)
    full = np.zeros((16, 2, 128, 16, 2, 8))
    full[:, 0, :, :, 0], full[:, 0, :, :, 1] = c, -s
    full[:, 1, :, :, 0], full[:, 1, :, :, 1] = s, c
    out["a"] = halves(full.reshape(16, 256, 256))
    num = r128[None, :, None] * r128[None, None, :] * (n // 128) + r128[None, :, None] * 16 * r16[:, None, None]
    c, s = unit(num, n, 1)
    out["b"] = halves(np.concatenate([np.concatenate([c, -s], 2), np.concatenate([s, c], 2)], 1))
    c, s = unit(r128[:, None] * r256[None, :], 32768, 1)
    out["base"] = np.stack([c, s]).astype(np.float32)
    c, s = unit(r16[:, None] * r128[None, :], n, 1)
    gl = np.stack([c, s], axis=1).astype(np.float32)
    out["gl"] = np.ascontiguousarray(np.broadcast_to(gl[..., None], gl.shape + (128,)))
    q, par, jj = np.meshgrid(np.arange(QC), np.arange(2), np.arange(RQ), indexing="ij")
    hh = 2 * (RQ * q + jj) + par
    hh = hh.reshape(QC, 2 * RQ)
    c, s = unit(hh[:, :, None] * r256[None, None, :], 256, 1)
    out["h"] = halves(np.concatenate([np.concatenate([c, -s], 2), np.concatenate([s, c], 2)], 1))
    e = r16[:, None] + 16 * r16[None, :]
    c, s = unit(hh.reshape(1, 256, 1) * e[:, None, :], 65536, 1)
    cj = np.zeros((16, 2, 256, 128), np.float32)
    cj[:, 0, :, :16], cj[:, 1, :, :16] = c, s
    out["cj"] = cj
    r = np.arange(256)
    c, s = unit(r[:, None] * r256[None, :], 256, -1)
    out["q"] = halves(np.block([[c, s], [-s, c]]) * 2.0**-27)
    return out


def cmul(ar, ai, br, bi):
    return ar * br - ai * bi, ar * bi + ai * br


def radix4(x, sign):
    (ar, ai), (br, bi), (cr, ci), (dr, di) = x
    pr, pi, mr, mi = ar + cr, ai + ci, ar - cr, ai - ci
    qr, qi, nr, ni = br + dr, bi + di, br - dr, bi - di
    if sign > 0:
        ur, ui = -ni, nr
        return [(pr + qr, pi + qi), (mr - ni, mi + nr), (pr - qr, pi - qi), (mr + ni, mi - nr)]
    return [(pr + qr, pi + qi), (mr + ni, mi - nr), (pr - qr, pi - qi), (mr - ni, mi + nr)]


def turn(x, power, sign):
    xr, xi = x
    power = power % 16
    if power == 0:
        return x
    if power == 4:
        return (-xi, xr) if sign > 0 else (xi, -xr)
    root = float(np.sqrt(0.5))
    if power == 2:
        return ((xr - xi) * root, (xr + xi) * root) if sign > 0 else ((xr + xi) * root, (xi - xr) * root)
    if power == 6:
        return ((-xr - xi) * root, (xr - xi) * root) if sign > 0 else ((xi - xr) * root, (-xr - xi) * root)
    c = float(np.cos(2 * np.pi * power / 16))
    s = float(sign * np.sin(2 * np.pi * power / 16))
    return (xr * c - xi * s, xr * s + xi * c)


def radix16(x, sign):
    inner = [radix4([x[4 * n1 + n2] for n1 in range(4)], sign) for n2 in range(4)]
    out = [None] * 16
    for k1 in range(4):
        column = radix4([turn(inner[n2][k1], n2 * k1, sign) for n2 in range(4)], sign)
        for k2 in range(4):
            out[k1 + 4 * k2] = column[k2]
    return out


def split(x):
    high = x.astype(bf16)
    return high, (x - high.astype(f32)).astype(bf16)


def dot(a, b):
    return lax.dot_general(a, b, (((1,), (0,)), ((), ())), preferred_element_type=f32)


def dot3(ah, al, bh, bl):
    return dot(ah, bh) + dot(al, bh) + dot(ah, bl)


def encode(x, inverse):
    a = jnp.abs(x) * inverse
    v = a * a + 1.0
    w = (a + v * lax.rsqrt(v)) * SHIFT
    w2 = w * w
    w4 = w2 * w2
    w8 = w4 * w4
    y = (w8 * w8) * w4
    return jnp.where(x < 0, -y, y)


def decode(y, half_scale):
    t = jnp.log(jnp.abs(y)) * (1.0 / POWER) + float(-np.log(SHIFT))
    w = jnp.exp(t)
    a = (w - jnp.exp(-t)) * half_scale
    return jnp.where(y < 0, -a, a)


def cos_sin(x):
    y = x * 0.5
    z = y * y
    s = 1.0 / 6227020800.0
    for factor in (-1.0 / 39916800.0, 1.0 / 362880.0, -1.0 / 5040.0, 1.0 / 120.0, -1.0 / 6.0, 1.0):
        s = s * z + factor
    s = s * y
    c = 1.0 / 479001600.0
    for factor in (-1.0 / 3628800.0, 1.0 / 40320.0, -1.0 / 720.0, 1.0 / 24.0, -0.5, 1.0):
        c = c * z + factor
    return 1.0 - 2.0 * s * s, 2.0 * s * c


def aligned(index, size):
    return pl.ds(pl.multiple_of(index * size, size), size)


def kernel(
    x_hbm, chirp_hbm, s1_ref, s2_ref, pw_hbm, gh_hbm, gl_hbm, c2_hbm, ah_hbm, al_hbm, bh_hbm, bl_hbm,
    base_hbm, lane_hbm, hh_hbm, hl_hbm, cj_hbm, qh_hbm, ql_hbm,
    out_hbm,
    x_v, d_v, pw_v, lhs_h, lhs_l, y_v, send1, recv1, send2, recv2, scale1_out, scale1, scale2_out, scale2,
    gh_v, gl_v, c2_v, ah_v, al_v, bh_v, bl_v, base_v, lane_v, hh_v, hl_v, cj_v, qh_v, ql_v,
    chirp_v, turn_v, wt_h, wt_l, u_v, v_v, z_v, xl_v, stage,
    load_sem, chirp_sem, tail_sems, scale_sems, send_sem1, recv_sem1, own_sem1, send_sem2, recv_sem2, own_sem2,
    out_sem,
):
    lane = lax.axis_index("fft")
    seg = lax.axis_index("seg")
    peer = lambda s: lax.rem(lane + s, LANES)

    def load(source, target, index):
        copy = pltpu.make_async_copy(source, target, load_sem.at[index])
        copy.start()
        return copy

    load_x = load(x_hbm, x_v.at[:, pl.ds(0, OWN)], 0)

    barrier = pltpu.get_barrier_semaphore()
    before, after = lax.rem(seg + SEGS - 1, SEGS), lax.rem(seg + 1, SEGS)

    def greet(s, carry):
        pl.semaphore_signal(barrier, inc=1, device_id={"fft": peer(s)}, device_id_type=MESH)
        return carry

    lax.fori_loop(1, LANES, greet, 0)
    pl.semaphore_signal(barrier, inc=1, device_id={"seg": before}, device_id_type=MESH)
    pl.semaphore_signal(barrier, inc=1, device_id={"seg": after}, device_id_type=MESH)

    load_pw = load(pw_hbm, pw_v, 1)
    load_g = [load(gh_hbm, gh_v, 2), load(gl_hbm, gl_v, 3), load(c2_hbm.at[lane], c2_v, 4)]

    pl.semaphore_wait(barrier, LANES + 1)
    tail = pltpu.make_async_remote_copy(
        src_ref=x_hbm.at[:, pl.ds(0, TAIL)],
        dst_ref=x_v.at[:, pl.ds(OWN, TAIL)],
        send_sem=tail_sems.at[0],
        recv_sem=tail_sems.at[1],
        device_id={"seg": before},
        device_id_type=MESH,
    )
    tail.start()
    load_x.wait()

    late = [
        load(ah_hbm, ah_v, 5), load(al_hbm, al_v, 6), load(bh_hbm, bh_v, 7), load(bl_hbm, bl_v, 8),
        load(base_hbm, base_v, 9), load(lane_hbm.at[lane], lane_v, 10), load(hh_hbm, hh_v, 11),
        load(hl_hbm, hl_v, 12), load(cj_hbm.at[lane], cj_v, 13), load(qh_hbm, qh_v, 14), load(ql_hbm, ql_v, 15),
    ]

    def chirp_copy(j):
        return pltpu.make_async_copy(chirp_hbm.at[:, j, :], chirp_v.at[j], chirp_sem.at[j])

    def chirp_start(j, carry):
        chirp_copy(j).start()
        return carry

    lax.fori_loop(0, 16, chirp_start, 0)

    tail.wait()

    @pl.when(seg == SEGS - 1)
    def _():
        x_v[:, pl.ds(OWN, TAIL)] = jnp.zeros((16, TAIL), bf16)

    def first_pass(t, energy):
        a_lo, half = t // 2, lax.rem(t, 2)
        x = []
        for a_hi in range(16):
            block = x_v[:, aligned((16 * a_hi + a_lo) * 2 + half, 128)].astype(f32)
            re, im = block[:8], block[8:]
            energy = energy + (re * re + im * im)
            x.append((re, im))
        x = radix16(x, -1)
        for e_lo in range(16):
            where = lane * 256 + a_lo * 16 + e_lo
            re, im = cmul(*x[e_lo], s1_ref[0, where], s1_ref[1, where])
            d_v[0, e_lo, a_lo, :, aligned(half, 128)] = re
            d_v[1, e_lo, a_lo, :, aligned(half, 128)] = im
        return energy

    energy = lax.fori_loop(0, 32, first_pass, jnp.zeros((8, 128), f32))

    def scale_of(energy):
        total = jnp.sum(jnp.sum(energy, axis=1, keepdims=True), axis=0, keepdims=True)
        mean = jnp.maximum(jnp.broadcast_to(total, (8, 128)), TINY)
        return mean * lax.rsqrt(mean) * (1.0 / KNEE)

    def send_scale(value, out_ref, in_ref, sems):
        out_ref[...] = value
        in_ref[lane] = value

        def send(s, carry):
            pltpu.make_async_remote_copy(
                src_ref=out_ref, dst_ref=in_ref.at[lane], send_sem=sems.at[0], recv_sem=sems.at[1],
                device_id={"fft": peer(s)}, device_id_type=MESH,
            ).start()
            return carry

        lax.fori_loop(1, LANES, send, 0)

    def wait_total(ref, sem):
        pltpu.make_async_copy(ref, ref, sem).wait()

    my_scale = scale_of(energy * 0.125)
    send_scale(my_scale, scale1_out, scale1, scale_sems.at[0])
    inverse = 1.0 / my_scale
    inverse = jnp.concatenate([inverse, inverse], axis=1)

    load_pw.wait()

    def second_pass(t, carry):
        e_lo, half = t // 2, lax.rem(t, 2)
        cols = aligned(half, 128)
        x = [(d_v[0, e_lo, a_lo, :, cols], d_v[1, e_lo, a_lo, :, cols]) for a_lo in range(16)]
        x = radix16(x, -1)
        for e_hi in range(16):
            re, im = cmul(*x[e_hi], pw_v[0, e_lo, e_hi, :, cols], pw_v[1, e_lo, e_hi, :, cols])
            d_v[0, e_lo, e_hi, :, cols] = re
            d_v[1, e_lo, e_hi, :, cols] = im
        return carry

    lax.fori_loop(0, 32, second_pass, 0)

    for copy in load_g:
        copy.wait()

    def chunk1(ref, jc, s):
        return ref.at[peer(s), pl.ds(jc * JC, JC)]

    def landing1(jc, source):
        return recv1.at[pl.ds(jc * JC, JC), source]

    rows = JC * 8

    def transform_b(t, carry):
        jc, half = t // 2, lax.rem(t, 2)
        for u in range(8):
            dest = peer(half * 8 + 1 + u)
            re = d_v[0, dest, pl.ds(jc * JC, JC)].reshape(rows, 256)
            im = d_v[1, dest, pl.ds(jc * JC, JC)].reshape(rows, 256)
            high, low = split(jnp.concatenate([re, im], axis=1))
            lhs_h[pl.ds(u * rows, rows), :] = high
            lhs_l[pl.ds(u * rows, rows), :] = low
        y_v[...] = dot3(lhs_h[...], lhs_l[...], gh_v[...], gl_v[...])
        cr, ci = c2_v[0][None], c2_v[1][None]
        for u in range(8):
            s = half * 8 + 1 + u
            block = y_v[pl.ds(u * rows, rows), :]
            re = block[:, :256].reshape(JC, 8, 256)
            im = block[:, 256:].reshape(JC, 8, 256)
            re, im = cmul(re, im, cr, ci)
            coded = jnp.concatenate([encode(re, inverse[None]), encode(im, inverse[None])], axis=1)
            send1[peer(s), pl.ds(jc * JC, JC)] = coded.astype(bf16)

            def remote():
                pltpu.make_async_remote_copy(
                    src_ref=chunk1(send1, jc, s), dst_ref=landing1(jc, lane),
                    send_sem=send_sem1, recv_sem=recv_sem1.at[jc],
                    device_id={"fft": peer(s)}, device_id_type=MESH,
                ).start()

            if u < 7:
                remote()
            else:
                pl.when(half == 0)(remote)

                @pl.when(half == 1)
                def _():
                    pltpu.make_async_copy(chunk1(send1, jc, s), landing1(jc, lane), own_sem1.at[jc]).start()

        return carry

    lax.fori_loop(0, 2 * NC, transform_b, 0)

    def response(j, carry):
        chirp_copy(j).wait()
        c, s = cos_sin(chirp_v[j])
        turn_v[0, j] = c
        turn_v[1, j] = s
        return carry

    lax.fori_loop(0, 16, response, 0)
    for copy in late:
        copy.wait()
    for part in range(2):
        cols = pl.ds(part * 128, 128)
        re, im = cmul(base_v[0, :, cols], base_v[1, :, cols], lane_v[0], lane_v[1])
        base_v[0, :, cols] = re
        base_v[1, :, cols] = im

    wait_total(scale1.at[pl.ds(0, LANES - 1)], scale_sems.at[0, 1])

    def middle(j, energy):
        half_scale = (scale1[...] * 0.5)[:, 0:1, :]
        half_scale = jnp.concatenate([half_scale, half_scale], axis=2)
        z = decode(recv1[j].astype(f32), half_scale).reshape(256, 256)
        zh, zl = split(z)
        o = dot3(ah_v[j], al_v[j], zh, zl)
        re, im = cmul(o[:128], o[128:], turn_v[0, j], turn_v[1, j])
        ph, pll = split(jnp.concatenate([re, im], axis=0))
        o = dot3(bh_v[j], bl_v[j], ph, pll)
        re, im = cmul(o[:128], o[128:], base_v[0], base_v[1])
        power = re * re + im * im
        energy = energy + jnp.sum(power.reshape(16, 8, 256), axis=0)
        both = jnp.concatenate([re.T, im.T], axis=0)
        high, low = split(both)
        wt_h[:, aligned(j, 128)] = high
        wt_l[:, aligned(j, 128)] = low
        return energy

    def middle_chunk(jc, energy):
        wait_total(recv1.at[pl.ds(jc * JC, JC), pl.ds(0, LANES - 1)], recv_sem1.at[jc])
        wait_total(landing1(jc, lane), own_sem1.at[jc])
        return lax.fori_loop(jc * JC, jc * JC + JC, middle, energy)

    energy = lax.fori_loop(0, NC, middle_chunk, jnp.zeros((8, 256), f32))
    my_scale = scale_of((energy[:, :128] + energy[:, 128:]) * (1.0 / 128.0))
    send_scale(my_scale, scale2_out, scale2, scale_sems.at[1])
    inverse2 = (1.0 / my_scale)[0:1, :]

    def post(q, carry):
        def columns(block, inner):
            cols = aligned(block, 512)
            u_v[:, cols] = dot3(hh_v[q], hl_v[q], wt_h[:, cols], wt_l[:, cols])
            return inner

        lax.fori_loop(0, 4, columns, 0)

        def rows_of(rt, inner):
            top = aligned(rt, 8)
            low = pl.ds(pl.multiple_of(2 * RQ + rt * 8, 8), 8)
            table = pl.ds(pl.multiple_of(q * 2 * RQ + rt * 8, 8), 8)
            tr, ti = cj_v[0, table, :], cj_v[1, table, :]
            x = []
            for j in range(16):
                cols = pl.ds(j * 128, 128)
                x.append(cmul(u_v[top, cols], u_v[low, cols], tr[:, j : j + 1], ti[:, j : j + 1]))
            x = radix16(x, 1)
            for l in range(16):
                re, im = cmul(*x[l], s2_ref[0, lane * 16 + l], s2_ref[1, lane * 16 + l])
                v_v[l, 0, top, :] = re
                v_v[l, 1, top, :] = im
            return inner

        lax.fori_loop(0, 2 * RQ // 8, rows_of, 0)

        def code(s, inner):
            dest = peer(s)
            send2[dest, q] = encode(v_v[dest], inverse2[None]).astype(bf16)

            @pl.when(s < LANES)
            def _():
                pltpu.make_async_remote_copy(
                    src_ref=send2.at[dest, q], dst_ref=recv2.at[q, lane],
                    send_sem=send_sem2, recv_sem=recv_sem2.at[q],
                    device_id={"fft": dest}, device_id_type=MESH,
                ).start()

            @pl.when(s == LANES)
            def _():
                pltpu.make_async_copy(send2.at[dest, q], recv2.at[q, lane], own_sem2.at[q]).start()

            return inner

        return lax.fori_loop(1, LANES + 1, code, carry)

    lax.fori_loop(0, QC, post, 0)

    wait_total(scale2.at[pl.ds(0, LANES - 1)], scale_sems.at[1, 1])

    def out_copy(q):
        return pltpu.make_async_copy(stage.at[lax.rem(q, 2)], out_hbm.at[:, pl.ds(q * RQ, RQ), :], out_sem.at[q])

    def final(q, carry):
        wait_total(recv2.at[q, pl.ds(0, LANES - 1)], recv_sem2.at[q])
        wait_total(recv2.at[q, lane], own_sem2.at[q])

        def undo(source, inner):
            half_scale = (scale2[source] * 0.5)[0:1, :]
            z_v[source] = decode(recv2[q, source].astype(f32), half_scale[None])
            return inner

        lax.fori_loop(0, LANES, undo, 0)

        def rows_of(rt, inner):
            top = aligned(rt, 8)
            par, jt = rt // (RQ // 8), lax.rem(rt, RQ // 8)
            x = radix16([(z_v[s, 0, top, :], z_v[s, 1, top, :]) for s in range(16)], 1)
            for t in range(15):
                where = pl.ds(pl.multiple_of(t * RQ + jt * 8, 8), 8)
                xl_v[where, aligned(par, 128)] = x[t][0]
                xl_v[where, aligned(par + 2, 128)] = x[t][1]
            return inner

        lax.fori_loop(0, 2 * RQ // 8, rows_of, 0)

        @pl.when(q >= 2)
        def _():
            out_copy(q - 2).wait()

        def channels(block, inner):
            high, low = split(xl_v[aligned(block, 5 * RQ), :])
            y = dot3(high, low, qh_v[...], ql_v[...])
            re, im = y[:, :256], y[:, 256:]
            stage[lax.rem(q, 2), pl.ds(block * 5, 5)] = (re * re + im * im).reshape(5, RQ, 256)
            return inner

        lax.fori_loop(0, 3, channels, 0)
        out_copy(q).start()
        return carry

    lax.fori_loop(0, QC, final, 0)
    out_copy(QC - 2).wait()
    out_copy(QC - 1).wait()

    wait_total(scale1.at[pl.ds(0, LANES - 1)], scale_sems.at[0, 0])
    wait_total(scale2.at[pl.ds(0, LANES - 1)], scale_sems.at[1, 0])
    wait_total(send1.at[pl.ds(0, LANES - 1)], send_sem1)
    wait_total(send2.at[pl.ds(0, LANES - 1)], send_sem2)


def on_device(baseband, chirp_phase):
    t = tables()
    constants = [
        t["s1"], t["s2"], t["pw"], *t["g"], t["c2"], *t["a"], *t["b"], t["base"], t["gl"], *t["h"], t["cj"], *t["q"],
    ]
    constants = [jnp.asarray(c) for c in constants]
    anywhere = pl.BlockSpec(memory_space=pl.ANY)
    scalars = pl.BlockSpec(memory_space=pltpu.SMEM)
    v = lambda shape, kind=f32: pltpu.VMEM(shape, kind)
    dma = pltpu.SemaphoreType.DMA
    out = pl.pallas_call(
        kernel,
        out_shape=jax.ShapeDtypeStruct((15, 128, 256), f32),
        in_specs=[anywhere, anywhere, scalars, scalars] + [anywhere] * (len(constants) - 2),
        out_specs=anywhere,
        scratch_shapes=[
            v((16, COLS), bf16), v((2, 16, 16, 8, 256)), v((2, 16, 16, 8, 256)),
            v((JC * 64, 512), bf16), v((JC * 64, 512), bf16), v((JC * 64, 512)),
            v((16, 16, 16, 256), bf16), v((16, 16, 16, 256), bf16),
            v((16, QC, 2, 2 * RQ, 128), bf16), v((QC, 16, 2, 2 * RQ, 128), bf16),
            v((8, 128)), v((16, 8, 128)), v((8, 128)), v((16, 8, 128)),
            v((512, 512), bf16), v((512, 512), bf16), v((2, 8, 256)),
            v((16, 256, 256), bf16), v((16, 256, 256), bf16), v((16, 256, 256), bf16), v((16, 256, 256), bf16),
            v((2, 128, 256)), v((2, 128, 128)),
            v((QC, 4 * RQ, 512), bf16), v((QC, 4 * RQ, 512), bf16), v((2, 256, 128)),
            v((512, 512), bf16), v((512, 512), bf16),
            v((16, 128, 256)), v((2, 16, 128, 256)),
            v((512, 2048), bf16), v((512, 2048), bf16), v((4 * RQ, 2048)),
            v((16, 2, 2 * RQ, 128)), v((16, 2, 2 * RQ, 128)), v((15 * RQ, 512)), v((2, 15, RQ, 256)),
            dma((16,)), dma((16,)), dma((2,)), dma((2, 2)), dma, dma((NC,)), dma((NC,)), dma, dma((QC,)),
            dma((QC,)), dma((QC,)),
        ],
        compiler_params=pltpu.CompilerParams(
            collective_id=0, has_side_effects=True, vmem_limit_bytes=60 * 1024 * 1024
        ),
        name="dedisperse",
    )(baseband.reshape(16, OWN), chirp_phase.reshape(128, 16, 256), *constants)
    return out.reshape(1, 15, 1, 128, 256)


def solution(mesh):
    return jax.shard_map(
        on_device,
        mesh=mesh,
        in_specs=(P("seg", "fft", None, None, None, None), P("fft", None, None, None)),
        out_specs=P("seg", None, "fft", None, None),
        check_vma=False,
    )
```

time: 663 us -> 127 us (0.19)
  the two profiles are of different devices: /device:TPU:26 before, /device:TPU:1 now
where the time goes in v1:
time: 127 us
  Pallas kernels  124 us (98%)
  local copies, waits for them, and re-layouts  2.99 us (2%)
    pallas_call x1, Pallas kernels, on_device(): pl.pallas_call(kernel, out_shape=jax.ShapeDtypeStruct((15, 128, 256), f32...  124 us
    unnamed x1, local copies, waits for them, and re-layouts  2.99 us

profile of v1, /device:TPU:1, one launch (start us, length us, event | category | flops | bytes accessed | tf_op | source)
XLA Modules:
  0.0 126.9 jit_solution(12841222840983731396)
XLA Ops:
  0.0 123.9 %dedisperse.1 = f32[15,128,256]{2,1,0:T(8,128)} custom-call(bf16[16,61440]{1,0:T(8,128)(2,1)} %bitcast.7, f32[128,16,256]{2,1,0:T(8,128)} %bitcast.6, f32[2,4096]{1,0:T(2,128)} %constant.34.clone.s1_ref, f32[2,256]{1,0:T(2,128)} %constant.35.clone.s2_ref, f32[2,16,16,8,256]{4,3,2,1,0:T(8,128)} %constant.36.clone.pw_hbm, ...), custom_call_target="tpu_custom_call" | custom-call | tf_op jit(solution)/shard_map/dedisperse/pallas_call | solution.py:522
  124.0 3.0 %copy.22 = f32[1,15,1,128,256]{4,3,2,1,0:T(8,128)} copy(f32[1,15,1,128,256]{4,3,2,1,0:T(8,128)} %bitcast.5) | data formatting | bytes 3932160

commit v2 on v1

--- a/solution.py
+++ b/solution.py
@@ -15,10 +15,10 @@
 OWN = 61440
 TAIL = 4096
 COLS = OWN + TAIL
-JC = 4
+JC = 2
 NC = 16 // JC
-QC = 4
-RQ = 32
+QC = 8
+RQ = 16
 KNEE = 4.0
 POWER = 20
 SHIFT = 2.0**-6.25
@@ -83,7 +83,8 @@
     hh = 2 * (RQ * q + jj) + par
     hh = hh.reshape(QC, 2 * RQ)
     c, s = unit(hh[:, :, None] * r256[None, None, :], 256, 1)
-    out["h"] = halves(np.concatenate([np.concatenate([c, -s], 2), np.concatenate([s, c], 2)], 1))
+    both = np.concatenate([np.concatenate([c, -s], 2), np.concatenate([s, c], 2)], 1)
+    out["h"] = halves(both.reshape(512, 512))
     e = r16[:, None] + 16 * r16[None, :]
     c, s = unit(hh.reshape(1, 256, 1) * e[:, None, :], 65536, 1)
     cj = np.zeros((16, 2, 256, 128), np.float32)
@@ -190,13 +191,19 @@
     out_hbm,
     x_v, d_v, pw_v, lhs_h, lhs_l, y_v, send1, recv1, send2, recv2, scale1_out, scale1, scale2_out, scale2,
     gh_v, gl_v, c2_v, ah_v, al_v, bh_v, bl_v, base_v, lane_v, hh_v, hl_v, cj_v, qh_v, ql_v,
-    chirp_v, turn_v, wt_h, wt_l, u_v, v_v, z_v, xl_v, stage,
-    load_sem, chirp_sem, tail_sems, scale_sems, send_sem1, recv_sem1, own_sem1, send_sem2, recv_sem2, own_sem2,
+    chirp_v, turn_v, u_v, v_v, z_v, xl_v, stage,
+    load_sem, chirp_sem, head_sems, scale_sems, send_sem1, recv_sem1, own_sem1, send_sem2, recv_sem2, own_sem2,
     out_sem,
 ):
     lane = lax.axis_index("fft")
     seg = lax.axis_index("seg")
-    peer = lambda s: lax.rem(lane + s, LANES)
+    lane_x, lane_z = lane // 4, lax.rem(lane, 4)
+
+    def peer(turn_index):
+        step_z, step_x = (2, 1, 3, 0)[turn_index // 4], (turn_index + 1) % 4
+        return lax.rem(lane_x + step_x, 4) * 4 + lax.rem(lane_z + step_z, 4)
+
+    before, after = lax.rem(seg + SEGS - 1, SEGS), lax.rem(seg + 1, SEGS)
 
     def load(source, target, index):
         copy = pltpu.make_async_copy(source, target, load_sem.at[index])
@@ -206,30 +213,39 @@
     load_x = load(x_hbm, x_v.at[:, pl.ds(0, OWN)], 0)
 
     barrier = pltpu.get_barrier_semaphore()
-    before, after = lax.rem(seg + SEGS - 1, SEGS), lax.rem(seg + 1, SEGS)
-
-    def greet(s, carry):
+
+    @pl.when(seg < SEGS - 1)
+    def _():
+        pl.semaphore_signal(barrier, inc=1, device_id={"seg": after}, device_id_type=MESH)
+
+    for s in range(LANES - 1):
         pl.semaphore_signal(barrier, inc=1, device_id={"fft": peer(s)}, device_id_type=MESH)
-        return carry
-
-    lax.fori_loop(1, LANES, greet, 0)
-    pl.semaphore_signal(barrier, inc=1, device_id={"seg": before}, device_id_type=MESH)
-    pl.semaphore_signal(barrier, inc=1, device_id={"seg": after}, device_id_type=MESH)
-
     load_pw = load(pw_hbm, pw_v, 1)
     load_g = [load(gh_hbm, gh_v, 2), load(gl_hbm, gl_v, 3), load(c2_hbm.at[lane], c2_v, 4)]
-
-    pl.semaphore_wait(barrier, LANES + 1)
-    tail = pltpu.make_async_remote_copy(
-        src_ref=x_hbm.at[:, pl.ds(0, TAIL)],
-        dst_ref=x_v.at[:, pl.ds(OWN, TAIL)],
-        send_sem=tail_sems.at[0],
-        recv_sem=tail_sems.at[1],
-        device_id={"seg": before},
-        device_id_type=MESH,
+    head = pltpu.make_async_remote_copy(
+        src_ref=x_hbm.at[:, pl.ds(0, TAIL)], dst_ref=x_v.at[:, pl.ds(OWN, TAIL)],
+        send_sem=head_sems.at[0], recv_sem=head_sems.at[1],
+        device_id={"seg": before}, device_id_type=MESH,
     )
-    tail.start()
+
+    @pl.when(seg > 0)
+    def _():
+        pl.semaphore_wait(barrier, LANES)
+        head.start()
+
+    @pl.when(seg == 0)
+    def _():
+        pl.semaphore_wait(barrier, LANES - 1)
+
     load_x.wait()
+
+    @pl.when(seg < SEGS - 1)
+    def _():
+        head.wait_recv()
+
+    @pl.when(seg == SEGS - 1)
+    def _():
+        x_v[:, pl.ds(OWN, TAIL)] = jnp.zeros((16, TAIL), bf16)
 
     late = [
         load(ah_hbm, ah_v, 5), load(al_hbm, al_v, 6), load(bh_hbm, bh_v, 7), load(bl_hbm, bl_v, 8),
@@ -245,12 +261,6 @@
         return carry
 
     lax.fori_loop(0, 16, chirp_start, 0)
-
-    tail.wait()
-
-    @pl.when(seg == SEGS - 1)
-    def _():
-        x_v[:, pl.ds(OWN, TAIL)] = jnp.zeros((16, TAIL), bf16)
 
     def first_pass(t, energy):
         a_lo, half = t // 2, lax.rem(t, 2)
@@ -279,20 +289,16 @@
         out_ref[...] = value
         in_ref[lane] = value
 
-        def send(s, carry):
+        for s in range(LANES - 1):
             pltpu.make_async_remote_copy(
                 src_ref=out_ref, dst_ref=in_ref.at[lane], send_sem=sems.at[0], recv_sem=sems.at[1],
                 device_id={"fft": peer(s)}, device_id_type=MESH,
             ).start()
-            return carry
-
-        lax.fori_loop(1, LANES, send, 0)
 
     def wait_total(ref, sem):
         pltpu.make_async_copy(ref, ref, sem).wait()
 
     my_scale = scale_of(energy * 0.125)
-    send_scale(my_scale, scale1_out, scale1, scale_sems.at[0])
     inverse = 1.0 / my_scale
     inverse = jnp.concatenate([inverse, inverse], axis=1)
 
@@ -313,6 +319,7 @@
 
     for copy in load_g:
         copy.wait()
+    send_scale(my_scale, scale1_out, scale1, scale_sems.at[0])
 
     def chunk1(ref, jc, s):
         return ref.at[peer(s), pl.ds(jc * JC, JC)]
@@ -322,10 +329,9 @@
 
     rows = JC * 8
 
-    def transform_b(t, carry):
-        jc, half = t // 2, lax.rem(t, 2)
-        for u in range(8):
-            dest = peer(half * 8 + 1 + u)
+    def transform_b(jc, carry):
+        for u in range(LANES):
+            dest = peer(u)
             re = d_v[0, dest, pl.ds(jc * JC, JC)].reshape(rows, 256)
             im = d_v[1, dest, pl.ds(jc * JC, JC)].reshape(rows, 256)
             high, low = split(jnp.concatenate([re, im], axis=1))
@@ -333,34 +339,25 @@
             lhs_l[pl.ds(u * rows, rows), :] = low
         y_v[...] = dot3(lhs_h[...], lhs_l[...], gh_v[...], gl_v[...])
         cr, ci = c2_v[0][None], c2_v[1][None]
-        for u in range(8):
-            s = half * 8 + 1 + u
+        for u in range(LANES):
+            dest = peer(u)
             block = y_v[pl.ds(u * rows, rows), :]
             re = block[:, :256].reshape(JC, 8, 256)
             im = block[:, 256:].reshape(JC, 8, 256)
             re, im = cmul(re, im, cr, ci)
             coded = jnp.concatenate([encode(re, inverse[None]), encode(im, inverse[None])], axis=1)
-            send1[peer(s), pl.ds(jc * JC, JC)] = coded.astype(bf16)
-
-            def remote():
+            send1[dest, pl.ds(jc * JC, JC)] = coded.astype(bf16)
+            if u < LANES - 1:
                 pltpu.make_async_remote_copy(
-                    src_ref=chunk1(send1, jc, s), dst_ref=landing1(jc, lane),
+                    src_ref=chunk1(send1, jc, u), dst_ref=landing1(jc, lane),
                     send_sem=send_sem1, recv_sem=recv_sem1.at[jc],
-                    device_id={"fft": peer(s)}, device_id_type=MESH,
+                    device_id={"fft": dest}, device_id_type=MESH,
                 ).start()
-
-            if u < 7:
-                remote()
             else:
-                pl.when(half == 0)(remote)
-
-                @pl.when(half == 1)
-                def _():
-                    pltpu.make_async_copy(chunk1(send1, jc, s), landing1(jc, lane), own_sem1.at[jc]).start()
-
+                pltpu.make_async_copy(chunk1(send1, jc, u), landing1(jc, lane), own_sem1.at[jc]).start()
         return carry
 
-    lax.fori_loop(0, 2 * NC, transform_b, 0)
+    lax.fori_loop(0, NC, transform_b, 0)
 
     def response(j, carry):
         chirp_copy(j).wait()
@@ -380,7 +377,7 @@
 
     wait_total(scale1.at[pl.ds(0, LANES - 1)], scale_sems.at[0, 1])
 
-    def middle(j, energy):
+    def middle(j):
         half_scale = (scale1[...] * 0.5)[:, 0:1, :]
         half_scale = jnp.concatenate([half_scale, half_scale], axis=2)
         z = decode(recv1[j].astype(f32), half_scale).reshape(256, 256)
@@ -390,18 +387,20 @@
         ph, pll = split(jnp.concatenate([re, im], axis=0))
         o = dot3(bh_v[j], bl_v[j], ph, pll)
         re, im = cmul(o[:128], o[128:], base_v[0], base_v[1])
-        power = re * re + im * im
-        energy = energy + jnp.sum(power.reshape(16, 8, 256), axis=0)
-        both = jnp.concatenate([re.T, im.T], axis=0)
-        high, low = split(both)
-        wt_h[:, aligned(j, 128)] = high
-        wt_l[:, aligned(j, 128)] = low
-        return energy
+        power = jnp.sum((re * re + im * im).reshape(16, 8, 256), axis=0)
+        return jnp.concatenate([re.T, im.T], axis=0), power
 
     def middle_chunk(jc, energy):
         wait_total(recv1.at[pl.ds(jc * JC, JC), pl.ds(0, LANES - 1)], recv_sem1.at[jc])
         wait_total(landing1(jc, lane), own_sem1.at[jc])
-        return lax.fori_loop(jc * JC, jc * JC + JC, middle, energy)
+        parts = []
+        for r in range(JC):
+            part, power = middle(jc * JC + r)
+            parts.append(part)
+            energy = energy + power
+        high, low = split(jnp.concatenate(parts, axis=1))
+        u_v[:, aligned(jc, JC * 128)] = dot3(hh_v[...], hl_v[...], high, low)
+        return energy
 
     energy = lax.fori_loop(0, NC, middle_chunk, jnp.zeros((8, 256), f32))
     my_scale = scale_of((energy[:, :128] + energy[:, 128:]) * (1.0 / 128.0))
@@ -409,22 +408,16 @@
     inverse2 = (1.0 / my_scale)[0:1, :]
 
     def post(q, carry):
-        def columns(block, inner):
-            cols = aligned(block, 512)
-            u_v[:, cols] = dot3(hh_v[q], hl_v[q], wt_h[:, cols], wt_l[:, cols])
-            return inner
-
-        lax.fori_loop(0, 4, columns, 0)
-
         def rows_of(rt, inner):
             top = aligned(rt, 8)
-            low = pl.ds(pl.multiple_of(2 * RQ + rt * 8, 8), 8)
+            high = pl.ds(pl.multiple_of(q * 4 * RQ + rt * 8, 8), 8)
+            low = pl.ds(pl.multiple_of(q * 4 * RQ + 2 * RQ + rt * 8, 8), 8)
             table = pl.ds(pl.multiple_of(q * 2 * RQ + rt * 8, 8), 8)
             tr, ti = cj_v[0, table, :], cj_v[1, table, :]
             x = []
             for j in range(16):
                 cols = pl.ds(j * 128, 128)
-                x.append(cmul(u_v[top, cols], u_v[low, cols], tr[:, j : j + 1], ti[:, j : j + 1]))
+                x.append(cmul(u_v[high, cols], u_v[low, cols], tr[:, j : j + 1], ti[:, j : j + 1]))
             x = radix16(x, 1)
             for l in range(16):
                 re, im = cmul(*x[l], s2_ref[0, lane * 16 + l], s2_ref[1, lane * 16 + l])
@@ -434,25 +427,18 @@
 
         lax.fori_loop(0, 2 * RQ // 8, rows_of, 0)
 
-        def code(s, inner):
+        for s in range(LANES):
             dest = peer(s)
             send2[dest, q] = encode(v_v[dest], inverse2[None]).astype(bf16)
-
-            @pl.when(s < LANES)
-            def _():
+            if s < LANES - 1:
                 pltpu.make_async_remote_copy(
                     src_ref=send2.at[dest, q], dst_ref=recv2.at[q, lane],
                     send_sem=send_sem2, recv_sem=recv_sem2.at[q],
                     device_id={"fft": dest}, device_id_type=MESH,
                 ).start()
-
-            @pl.when(s == LANES)
-            def _():
+            else:
                 pltpu.make_async_copy(send2.at[dest, q], recv2.at[q, lane], own_sem2.at[q]).start()
-
-            return inner
-
-        return lax.fori_loop(1, LANES + 1, code, carry)
+        return carry
 
     lax.fori_loop(0, QC, post, 0)
 
@@ -503,6 +489,10 @@
     out_copy(QC - 2).wait()
     out_copy(QC - 1).wait()
 
+    @pl.when(seg > 0)
+    def _():
+        head.wait_send()
+
     wait_total(scale1.at[pl.ds(0, LANES - 1)], scale_sems.at[0, 0])
     wait_total(scale2.at[pl.ds(0, LANES - 1)], scale_sems.at[1, 0])
     wait_total(send1.at[pl.ds(0, LANES - 1)], send_sem1)
@@ -510,6 +500,7 @@
 
 
 def on_device(baseband, chirp_phase):
+    own = baseband.reshape(16, OWN)
     t = tables()
     constants = [
         t["s1"], t["s2"], t["pw"], *t["g"], t["c2"], *t["a"], *t["b"], t["base"], t["gl"], *t["h"], t["cj"], *t["q"],
@@ -526,17 +517,17 @@
         out_specs=anywhere,
         scratch_shapes=[
             v((16, COLS), bf16), v((2, 16, 16, 8, 256)), v((2, 16, 16, 8, 256)),
-            v((JC * 64, 512), bf16), v((JC * 64, 512), bf16), v((JC * 64, 512)),
+            v((JC * 128, 512), bf16), v((JC * 128, 512), bf16), v((JC * 128, 512)),
             v((16, 16, 16, 256), bf16), v((16, 16, 16, 256), bf16),
             v((16, QC, 2, 2 * RQ, 128), bf16), v((QC, 16, 2, 2 * RQ, 128), bf16),
             v((8, 128)), v((16, 8, 128)), v((8, 128)), v((16, 8, 128)),
             v((512, 512), bf16), v((512, 512), bf16), v((2, 8, 256)),
             v((16, 256, 256), bf16), v((16, 256, 256), bf16), v((16, 256, 256), bf16), v((16, 256, 256), bf16),
             v((2, 128, 256)), v((2, 128, 128)),
-            v((QC, 4 * RQ, 512), bf16), v((QC, 4 * RQ, 512), bf16), v((2, 256, 128)),
+            v((512, 512), bf16), v((512, 512), bf16), v((2, 256, 128)),
             v((512, 512), bf16), v((512, 512), bf16),
             v((16, 128, 256)), v((2, 16, 128, 256)),
-            v((512, 2048), bf16), v((512, 2048), bf16), v((4 * RQ, 2048)),
+            v((512, 2048)),
             v((16, 2, 2 * RQ, 128)), v((16, 2, 2 * RQ, 128)), v((15 * RQ, 512)), v((2, 15, RQ, 256)),
             dma((16,)), dma((16,)), dma((2,)), dma((2, 2)), dma, dma((NC,)), dma((NC,)), dma, dma((QC,)),
             dma((QC,)), dma((QC,)),
@@ -545,7 +536,7 @@
             collective_id=0, has_side_effects=True, vmem_limit_bytes=60 * 1024 * 1024
         ),
         name="dedisperse",
-    )(baseband.reshape(16, OWN), chirp_phase.reshape(128, 16, 256), *constants)
+    )(own, chirp_phase.reshape(128, 16, 256), *constants)
     return out.reshape(1, 15, 1, 128, 256)
 
 

time: 127 us -> 118 us (0.929)
  Pallas kernels: 124 us -> 115 us
    pallas_call x1, Pallas kernels: 124 us -> 115 us  [on_device(): pl.pallas_call(kernel, out_shape=jax.ShapeDtypeStruct((15, 128, 256), f32...]
where the time goes in v2:
time: 118 us
  Pallas kernels  115 us (97%)
  local copies, waits for them, and re-layouts  2.99 us (3%)
    pallas_call x1, Pallas kernels, on_device(): pl.pallas_call(kernel, out_shape=jax.ShapeDtypeStruct((15, 128, 256), f32...  115 us
    unnamed x1, local copies, waits for them, and re-layouts  2.99 us

profile of v2, /device:TPU:1, one launch (start us, length us, event | category | flops | bytes accessed | tf_op | source)
XLA Modules:
  0.0 118.3 jit_solution(16709956168376423730)
XLA Ops:
  0.0 115.3 %dedisperse.1 = f32[15,128,256]{2,1,0:T(8,128)} custom-call(bf16[16,61440]{1,0:T(8,128)(2,1)} %bitcast.7, f32[128,16,256]{2,1,0:T(8,128)} %bitcast.6, f32[2,4096]{1,0:T(2,128)} %constant.34.clone.s1_ref, f32[2,256]{1,0:T(2,128)} %constant.35.clone.s2_ref, f32[2,16,16,8,256]{4,3,2,1,0:T(8,128)} %constant.36.clone.pw_hbm, ...), custom_call_target="tpu_custom_call" | custom-call | tf_op jit(solution)/shard_map/dedisperse/pallas_call | solution.py:513
  115.3 3.0 %copy.22 = f32[1,15,1,128,256]{4,3,2,1,0:T(8,128)} copy(f32[1,15,1,128,256]{4,3,2,1,0:T(8,128)} %bitcast.5) | data formatting | bytes 3932160

commit v3 on v2

--- a/solution.py
+++ b/solution.py
@@ -53,7 +53,11 @@
     )
     out["s1"] = np.stack([c, s]).astype(np.float32).reshape(2, -1)
     c, s = unit(r16[:, None] * r16[None, :], 256, 1)
-    out["s2"] = np.stack([c, s]).astype(np.float32).reshape(2, -1)
+    out["s2"] = np.stack([c, s])
+    scalars = np.zeros((16, 2, 640), np.float32)
+    scalars[:, :, :256] = out["s1"].reshape(2, 16, 256).transpose(1, 0, 2)
+    scalars[:, :, 512:528] = out["s2"].transpose(1, 0, 2)
+    out["scalars"] = scalars
     e = r16[:, None] + 16 * r16[None, :]
     ib = 16 * np.arange(8)[:, None] + 128 * r256[None, :]
     c, s = unit(e[:, :, None, None] * ib[None, None], n, -1)
@@ -186,10 +190,10 @@
 
 
 def kernel(
-    x_hbm, chirp_hbm, s1_ref, s2_ref, pw_hbm, gh_hbm, gl_hbm, c2_hbm, ah_hbm, al_hbm, bh_hbm, bl_hbm,
+    x_hbm, chirp_hbm, scalars_hbm, pw_hbm, gh_hbm, gl_hbm, c2_hbm, ah_hbm, al_hbm, bh_hbm, bl_hbm,
     base_hbm, lane_hbm, hh_hbm, hl_hbm, cj_hbm, qh_hbm, ql_hbm,
     out_hbm,
-    x_v, d_v, pw_v, lhs_h, lhs_l, y_v, send1, recv1, send2, recv2, scale1_out, scale1, scale2_out, scale2,
+    scalars, x_v, d_v, pw_v, lhs_h, lhs_l, y_v, send1, recv1, send2, recv2, scale1_out, scale1, scale2_out, scale2,
     gh_v, gl_v, c2_v, ah_v, al_v, bh_v, bl_v, base_v, lane_v, hh_v, hl_v, cj_v, qh_v, ql_v,
     chirp_v, turn_v, u_v, v_v, z_v, xl_v, stage,
     load_sem, chirp_sem, head_sems, scale_sems, send_sem1, recv_sem1, own_sem1, send_sem2, recv_sem2, own_sem2,
@@ -220,6 +224,7 @@
 
     for s in range(LANES - 1):
         pl.semaphore_signal(barrier, inc=1, device_id={"fft": peer(s)}, device_id_type=MESH)
+    load_scalars = load(scalars_hbm.at[lane], scalars, 16)
     load_pw = load(pw_hbm, pw_v, 1)
     load_g = [load(gh_hbm, gh_v, 2), load(gl_hbm, gl_v, 3), load(c2_hbm.at[lane], c2_v, 4)]
     head = pltpu.make_async_remote_copy(
@@ -238,6 +243,7 @@
         pl.semaphore_wait(barrier, LANES - 1)
 
     load_x.wait()
+    load_scalars.wait()
 
     @pl.when(seg < SEGS - 1)
     def _():
@@ -272,8 +278,8 @@
             x.append((re, im))
         x = radix16(x, -1)
         for e_lo in range(16):
-            where = lane * 256 + a_lo * 16 + e_lo
-            re, im = cmul(*x[e_lo], s1_ref[0, where], s1_ref[1, where])
+            where = a_lo * 16 + e_lo
+            re, im = cmul(*x[e_lo], scalars[0, where], scalars[1, where])
             d_v[0, e_lo, a_lo, :, aligned(half, 128)] = re
             d_v[1, e_lo, a_lo, :, aligned(half, 128)] = im
         return energy
@@ -420,7 +426,7 @@
                 x.append(cmul(u_v[high, cols], u_v[low, cols], tr[:, j : j + 1], ti[:, j : j + 1]))
             x = radix16(x, 1)
             for l in range(16):
-                re, im = cmul(*x[l], s2_ref[0, lane * 16 + l], s2_ref[1, lane * 16 + l])
+                re, im = cmul(*x[l], scalars[0, 512 + l], scalars[1, 512 + l])
                 v_v[l, 0, top, :] = re
                 v_v[l, 1, top, :] = im
             return inner
@@ -474,14 +480,10 @@
         def _():
             out_copy(q - 2).wait()
 
-        def channels(block, inner):
-            high, low = split(xl_v[aligned(block, 5 * RQ), :])
-            y = dot3(high, low, qh_v[...], ql_v[...])
-            re, im = y[:, :256], y[:, 256:]
-            stage[lax.rem(q, 2), pl.ds(block * 5, 5)] = (re * re + im * im).reshape(5, RQ, 256)
-            return inner
-
-        lax.fori_loop(0, 3, channels, 0)
+        high, low = split(xl_v[...])
+        y = dot3(high, low, qh_v[...], ql_v[...])
+        re, im = y[:, :256], y[:, 256:]
+        stage[lax.rem(q, 2)] = (re * re + im * im).reshape(15, RQ, 256)
         out_copy(q).start()
         return carry
 
@@ -503,20 +505,19 @@
     own = baseband.reshape(16, OWN)
     t = tables()
     constants = [
-        t["s1"], t["s2"], t["pw"], *t["g"], t["c2"], *t["a"], *t["b"], t["base"], t["gl"], *t["h"], t["cj"], *t["q"],
+        t["scalars"], t["pw"], *t["g"], t["c2"], *t["a"], *t["b"], t["base"], t["gl"], *t["h"], t["cj"], *t["q"],
     ]
     constants = [jnp.asarray(c) for c in constants]
     anywhere = pl.BlockSpec(memory_space=pl.ANY)
-    scalars = pl.BlockSpec(memory_space=pltpu.SMEM)
     v = lambda shape, kind=f32: pltpu.VMEM(shape, kind)
     dma = pltpu.SemaphoreType.DMA
     out = pl.pallas_call(
         kernel,
         out_shape=jax.ShapeDtypeStruct((15, 128, 256), f32),
-        in_specs=[anywhere, anywhere, scalars, scalars] + [anywhere] * (len(constants) - 2),
+        in_specs=[anywhere] * (len(constants) + 2),
         out_specs=anywhere,
         scratch_shapes=[
-            v((16, COLS), bf16), v((2, 16, 16, 8, 256)), v((2, 16, 16, 8, 256)),
+            pltpu.SMEM((2, 640), f32), v((16, COLS), bf16), v((2, 16, 16, 8, 256)), v((2, 16, 16, 8, 256)),
             v((JC * 128, 512), bf16), v((JC * 128, 512), bf16), v((JC * 128, 512)),
             v((16, 16, 16, 256), bf16), v((16, 16, 16, 256), bf16),
             v((16, QC, 2, 2 * RQ, 128), bf16), v((QC, 16, 2, 2 * RQ, 128), bf16),
@@ -529,7 +530,7 @@
             v((16, 128, 256)), v((2, 16, 128, 256)),
             v((512, 2048)),
             v((16, 2, 2 * RQ, 128)), v((16, 2, 2 * RQ, 128)), v((15 * RQ, 512)), v((2, 15, RQ, 256)),
-            dma((16,)), dma((16,)), dma((2,)), dma((2, 2)), dma, dma((NC,)), dma((NC,)), dma, dma((QC,)),
+            dma((17,)), dma((16,)), dma((2,)), dma((2, 2)), dma, dma((NC,)), dma((NC,)), dma, dma((QC,)),
             dma((QC,)), dma((QC,)),
         ],
         compiler_params=pltpu.CompilerParams(

time: 118 us -> 117 us (level)
  Pallas kernels: 115 us -> 113 us
    pallas_call x1, Pallas kernels: 115 us -> 113 us  [on_device(): pl.pallas_call(kernel, out_shape=jax.ShapeDtypeStruct((15, 128, 256), f32...]
where the time goes in v3:
time: 117 us; the launch traced here: 116 us
  Pallas kernels  113 us (97%)
  local copies, waits for them, and re-layouts  2.99 us (3%)
    pallas_call x1, Pallas kernels, on_device(): pl.pallas_call(kernel, out_shape=jax.ShapeDtypeStruct((15, 128, 256), f32...  113 us
    unnamed x1, local copies, waits for them, and re-layouts  2.99 us

profile of v3, /device:TPU:1, one launch (start us, length us, event | category | flops | bytes accessed | tf_op | source)
XLA Modules:
  0.0 116.5 jit_solution(15162767307104853795)
XLA Ops:
  0.0 113.5 %dedisperse.1 = f32[15,128,256]{2,1,0:T(8,128)} custom-call(bf16[16,61440]{1,0:T(8,128)(2,1)} %bitcast.7, f32[128,16,256]{2,1,0:T(8,128)} %bitcast.6, f32[16,2,640]{2,1,0:T(2,128)} %constant.32.clone.scalars_hbm, f32[2,16,16,8,256]{4,3,2,1,0:T(8,128)} %constant.33.clone.pw_hbm, bf16[512,512]{1,0:T(8,128)(2,1)} %constant.34.clone.gh_hbm, ...), custom_call_target="tpu_custom_call" | custom-call | tf_op jit(solution)/shard_map/dedisperse/pallas_call | solution.py:514
  113.5 3.0 %copy.21 = f32[1,15,1,128,256]{4,3,2,1,0:T(8,128)} copy(f32[1,15,1,128,256]{4,3,2,1,0:T(8,128)} %bitcast.5) | data formatting | bytes 3932160

commit v4 on v3

--- a/solution.py
+++ b/solution.py
@@ -189,8 +189,36 @@
     return pl.ds(pl.multiple_of(index * size, size), size)
 
 
+def head_kernel(x_hbm, tail_hbm, sems):
+    seg = lax.axis_index("seg")
+    phase = lax.rem(seg, 4)
+    before, after = lax.rem(seg + SEGS - 1, SEGS), lax.rem(seg + 1, SEGS)
+    barrier = pltpu.get_barrier_semaphore()
+    head = pltpu.make_async_remote_copy(
+        src_ref=x_hbm.at[:, pl.ds(0, TAIL)], dst_ref=tail_hbm, send_sem=sems.at[0], recv_sem=sems.at[1],
+        device_id={"seg": before}, device_id_type=MESH,
+    )
+
+    @pl.when(phase != 3)
+    def _():
+        pl.semaphore_signal(barrier, inc=1, device_id={"seg": after}, device_id_type=MESH)
+
+    @pl.when(phase != 0)
+    def _():
+        pl.semaphore_wait(barrier, 1)
+        head.start()
+
+    @pl.when(phase != 3)
+    def _():
+        head.wait_recv()
+
+    @pl.when(phase != 0)
+    def _():
+        head.wait_send()
+
+
 def kernel(
-    x_hbm, chirp_hbm, scalars_hbm, pw_hbm, gh_hbm, gl_hbm, c2_hbm, ah_hbm, al_hbm, bh_hbm, bl_hbm,
+    x_hbm, tail_hbm, chirp_hbm, scalars_hbm, pw_hbm, gh_hbm, gl_hbm, c2_hbm, ah_hbm, al_hbm, bh_hbm, bl_hbm,
     base_hbm, lane_hbm, hh_hbm, hl_hbm, cj_hbm, qh_hbm, ql_hbm,
     out_hbm,
     scalars, x_v, d_v, pw_v, lhs_h, lhs_l, y_v, send1, recv1, send2, recv2, scale1_out, scale1, scale2_out, scale2,
@@ -207,6 +235,7 @@
         step_z, step_x = (2, 1, 3, 0)[turn_index // 4], (turn_index + 1) % 4
         return lax.rem(lane_x + step_x, 4) * 4 + lax.rem(lane_z + step_z, 4)
 
+    phase = lax.rem(seg, 4)
     before, after = lax.rem(seg + SEGS - 1, SEGS), lax.rem(seg + 1, SEGS)
 
     def load(source, target, index):
@@ -218,12 +247,14 @@
 
     barrier = pltpu.get_barrier_semaphore()
 
-    @pl.when(seg < SEGS - 1)
+    @pl.when((phase == 3) & (seg < SEGS - 1))
     def _():
         pl.semaphore_signal(barrier, inc=1, device_id={"seg": after}, device_id_type=MESH)
 
     for s in range(LANES - 1):
         pl.semaphore_signal(barrier, inc=1, device_id={"fft": peer(s)}, device_id_type=MESH)
+    load_tail = pltpu.make_async_copy(tail_hbm, x_v.at[:, pl.ds(OWN, TAIL)], load_sem.at[17])
+    pl.when(phase != 3)(load_tail.start)
     load_scalars = load(scalars_hbm.at[lane], scalars, 16)
     load_pw = load(pw_hbm, pw_v, 1)
     load_g = [load(gh_hbm, gh_v, 2), load(gl_hbm, gl_v, 3), load(c2_hbm.at[lane], c2_v, 4)]
@@ -232,22 +263,10 @@
         send_sem=head_sems.at[0], recv_sem=head_sems.at[1],
         device_id={"seg": before}, device_id_type=MESH,
     )
-
-    @pl.when(seg > 0)
-    def _():
-        pl.semaphore_wait(barrier, LANES)
-        head.start()
-
-    @pl.when(seg == 0)
-    def _():
-        pl.semaphore_wait(barrier, LANES - 1)
-
     load_x.wait()
     load_scalars.wait()
-
-    @pl.when(seg < SEGS - 1)
-    def _():
-        head.wait_recv()
+    pl.when(phase != 3)(load_tail.wait)
+    pl.when((phase == 3) & (seg < SEGS - 1))(head.wait_recv)
 
     @pl.when(seg == SEGS - 1)
     def _():
@@ -325,6 +344,16 @@
 
     for copy in load_g:
         copy.wait()
+
+    @pl.when((phase == 0) & (seg > 0))
+    def _():
+        pl.semaphore_wait(barrier, LANES)
+        head.start()
+
+    @pl.when((phase != 0) | (seg == 0))
+    def _():
+        pl.semaphore_wait(barrier, LANES - 1)
+
     send_scale(my_scale, scale1_out, scale1, scale_sems.at[0])
 
     def chunk1(ref, jc, s):
@@ -491,7 +520,7 @@
     out_copy(QC - 2).wait()
     out_copy(QC - 1).wait()
 
-    @pl.when(seg > 0)
+    @pl.when((phase == 0) & (seg > 0))
     def _():
         head.wait_send()
 
@@ -503,6 +532,17 @@
 
 def on_device(baseband, chirp_phase):
     own = baseband.reshape(16, OWN)
+    tail = pl.pallas_call(
+        head_kernel,
+        out_shape=jax.ShapeDtypeStruct((16, TAIL), bf16),
+        in_specs=[pl.BlockSpec(memory_space=pl.ANY)],
+        out_specs=pl.BlockSpec(memory_space=pl.ANY),
+        scratch_shapes=[pltpu.SemaphoreType.DMA((2,))],
+        compiler_params=pltpu.CompilerParams(
+            collective_id=0, has_side_effects=True, vmem_limit_bytes=60 * 1024 * 1024
+        ),
+        name="heads",
+    )(own)
     t = tables()
     constants = [
         t["scalars"], t["pw"], *t["g"], t["c2"], *t["a"], *t["b"], t["base"], t["gl"], *t["h"], t["cj"], *t["q"],
@@ -514,7 +554,7 @@
     out = pl.pallas_call(
         kernel,
         out_shape=jax.ShapeDtypeStruct((15, 128, 256), f32),
-        in_specs=[anywhere] * (len(constants) + 2),
+        in_specs=[anywhere] * (len(constants) + 3),
         out_specs=anywhere,
         scratch_shapes=[
             pltpu.SMEM((2, 640), f32), v((16, COLS), bf16), v((2, 16, 16, 8, 256)), v((2, 16, 16, 8, 256)),
@@ -530,14 +570,14 @@
             v((16, 128, 256)), v((2, 16, 128, 256)),
             v((512, 2048)),
             v((16, 2, 2 * RQ, 128)), v((16, 2, 2 * RQ, 128)), v((15 * RQ, 512)), v((2, 15, RQ, 256)),
-            dma((17,)), dma((16,)), dma((2,)), dma((2, 2)), dma, dma((NC,)), dma((NC,)), dma, dma((QC,)),
+            dma((18,)), dma((16,)), dma((2,)), dma((2, 2)), dma, dma((NC,)), dma((NC,)), dma, dma((QC,)),
             dma((QC,)), dma((QC,)),
         ],
         compiler_params=pltpu.CompilerParams(
-            collective_id=0, has_side_effects=True, vmem_limit_bytes=60 * 1024 * 1024
+            collective_id=1, has_side_effects=True, vmem_limit_bytes=60 * 1024 * 1024
         ),
         name="dedisperse",
-    )(own, chirp_phase.reshape(128, 16, 256), *constants)
+    )(own, tail, chirp_phase.reshape(128, 16, 256), *constants)
     return out.reshape(1, 15, 1, 128, 256)
 
 

time: 117 us -> 116 us (level); the launches traced: 116 us -> 114 us
  Pallas kernels: 113 us -> 111 us
    pallas_call x1, Pallas kernels: 113 us -> 99.9 us  [on_device(): pl.pallas_call(kernel, out_shape=jax.ShapeDtypeStruct((15, 128, 256), f32...]
    pallas_call x0 -> x1, Pallas kernels: none -> 11.4 us  [on_device(): pl.pallas_call(head_kernel, out_shape=jax.ShapeDtypeStruct((16, TAIL), bf...]
where the time goes in v4:
time: 116 us; the launch traced here: 114 us
  Pallas kernels  111 us (96%)
  local copies, waits for them, and re-layouts  2.99 us (3%)
    pallas_call x1, Pallas kernels, on_device(): pl.pallas_call(kernel, out_shape=jax.ShapeDtypeStruct((15, 128, 256), f32...  99.9 us
    pallas_call x1, Pallas kernels, on_device(): pl.pallas_call(head_kernel, out_shape=jax.ShapeDtypeStruct((16, TAIL), bf...  11.4 us
    unnamed x1, local copies, waits for them, and re-layouts  2.99 us

profile of v4, /device:TPU:1, one launch (start us, length us, event | category | flops | bytes accessed | tf_op | source)
XLA Modules:
  0.0 114.3 jit_solution(15943201380566125029)
XLA Ops:
  0.0 11.4 %heads.1.tail_hbm = bf16[16,4096]{1,0:T(8,128)(2,1)} custom-call(bf16[16,61440]{1,0:T(8,128)(2,1)} %bitcast.5), custom_call_target="tpu_custom_call" | custom-call | tf_op jit(solution)/shard_map/heads/pallas_call | solution.py:535
  11.4 99.9 %dedisperse.1 = f32[15,128,256]{2,1,0:T(8,128)} custom-call(bf16[16,61440]{1,0:T(8,128)(2,1)} %bitcast.6, bf16[16,4096]{1,0:T(8,128)(2,1)} %heads.1.tail_hbm, f32[128,16,256]{2,1,0:T(8,128)} %bitcast.8, f32[16,2,640]{2,1,0:T(2,128)} %constant.32.clone.scalars_hbm, f32[2,16,16,8,256]{4,3,2,1,0:T(8,128)} %constant.33.clone.pw_hbm, ...), custom_call_target="tpu_custom_call" | custom-call | tf_op jit(solution)/shard_map/dedisperse/pallas_call | solution.py:554
  111.3 3.0 %copy.21 = f32[1,15,1,128,256]{4,3,2,1,0:T(8,128)} copy(f32[1,15,1,128,256]{4,3,2,1,0:T(8,128)} %bitcast.7) | data formatting | bytes 3932160

commit v5 on v4

--- a/solution.py
+++ b/solution.py
@@ -258,15 +258,18 @@
     load_scalars = load(scalars_hbm.at[lane], scalars, 16)
     load_pw = load(pw_hbm, pw_v, 1)
     load_g = [load(gh_hbm, gh_v, 2), load(gl_hbm, gl_v, 3), load(c2_hbm.at[lane], c2_v, 4)]
-    head = pltpu.make_async_remote_copy(
-        src_ref=x_hbm.at[:, pl.ds(0, TAIL)], dst_ref=x_v.at[:, pl.ds(OWN, TAIL)],
-        send_sem=head_sems.at[0], recv_sem=head_sems.at[1],
-        device_id={"seg": before}, device_id_type=MESH,
-    )
+    piece = TAIL // 4
+    heads = [
+        pltpu.make_async_remote_copy(
+            src_ref=x_hbm.at[:, pl.ds(h * piece, piece)], dst_ref=x_v.at[:, pl.ds(OWN + h * piece, piece)],
+            send_sem=head_sems.at[0, h], recv_sem=head_sems.at[1, h],
+            device_id={"seg": before}, device_id_type=MESH,
+        )
+        for h in range(4)
+    ]
     load_x.wait()
     load_scalars.wait()
     pl.when(phase != 3)(load_tail.wait)
-    pl.when((phase == 3) & (seg < SEGS - 1))(head.wait_recv)
 
     @pl.when(seg == SEGS - 1)
     def _():
@@ -303,7 +306,10 @@
             d_v[1, e_lo, a_lo, :, aligned(half, 128)] = im
         return energy
 
-    energy = lax.fori_loop(0, 32, first_pass, jnp.zeros((8, 128), f32))
+    energy = jnp.zeros((8, 128), f32)
+    for h in range(4):
+        pl.when((phase == 3) & (seg < SEGS - 1))(heads[h].wait_recv)
+        energy = lax.fori_loop(8 * h, 8 * h + 8, first_pass, energy)
 
     def scale_of(energy):
         total = jnp.sum(jnp.sum(energy, axis=1, keepdims=True), axis=0, keepdims=True)
@@ -348,7 +354,8 @@
     @pl.when((phase == 0) & (seg > 0))
     def _():
         pl.semaphore_wait(barrier, LANES)
-        head.start()
+        for head in heads:
+            head.start()
 
     @pl.when((phase != 0) | (seg == 0))
     def _():
@@ -522,7 +529,8 @@
 
     @pl.when((phase == 0) & (seg > 0))
     def _():
-        head.wait_send()
+        for head in heads:
+            head.wait_send()
 
     wait_total(scale1.at[pl.ds(0, LANES - 1)], scale_sems.at[0, 0])
     wait_total(scale2.at[pl.ds(0, LANES - 1)], scale_sems.at[1, 0])
@@ -570,7 +578,7 @@
             v((16, 128, 256)), v((2, 16, 128, 256)),
             v((512, 2048)),
             v((16, 2, 2 * RQ, 128)), v((16, 2, 2 * RQ, 128)), v((15 * RQ, 512)), v((2, 15, RQ, 256)),
-            dma((18,)), dma((16,)), dma((2,)), dma((2, 2)), dma, dma((NC,)), dma((NC,)), dma, dma((QC,)),
+            dma((18,)), dma((16,)), dma((2, 4)), dma((2, 2)), dma, dma((NC,)), dma((NC,)), dma, dma((QC,)),
             dma((QC,)), dma((QC,)),
         ],
         compiler_params=pltpu.CompilerParams(

time: 116 us -> 117 us (level)
  the two profiles are of different devices: /device:TPU:1 before, /device:TPU:177 now
where the time goes in v5:
time: 117 us
  Pallas kernels  114 us (97%)
  local copies, waits for them, and re-layouts  2.99 us (3%)
    pallas_call x1, Pallas kernels, on_device(): pl.pallas_call(kernel, out_shape=jax.ShapeDtypeStruct((15, 128, 256), f32...  112 us
    unnamed x1, local copies, waits for them, and re-layouts  2.99 us

profile of v5, /device:TPU:177, one launch (start us, length us, event | category | flops | bytes accessed | tf_op | source)
XLA Modules:
  0.0 116.6 jit_solution(12574257337945646703)
XLA Ops:
  0.0 2.0 %heads.1.tail_hbm = bf16[16,4096]{1,0:T(8,128)(2,1)} custom-call(bf16[16,61440]{1,0:T(8,128)(2,1)} %bitcast.5), custom_call_target="tpu_custom_call" | custom-call | tf_op jit(solution)/shard_map/heads/pallas_call | solution.py:543
  2.0 111.6 %dedisperse.1 = f32[15,128,256]{2,1,0:T(8,128)} custom-call(bf16[16,61440]{1,0:T(8,128)(2,1)} %bitcast.6, bf16[16,4096]{1,0:T(8,128)(2,1)} %heads.1.tail_hbm, f32[128,16,256]{2,1,0:T(8,128)} %bitcast.8, f32[16,2,640]{2,1,0:T(2,128)} %constant.32.clone.scalars_hbm, f32[2,16,16,8,256]{4,3,2,1,0:T(8,128)} %constant.33.clone.pw_hbm, ...), custom_call_target="tpu_custom_call" | custom-call | tf_op jit(solution)/shard_map/dedisperse/pallas_call | solution.py:562
  113.6 3.0 %copy.21 = f32[1,15,1,128,256]{4,3,2,1,0:T(8,128)} copy(f32[1,15,1,128,256]{4,3,2,1,0:T(8,128)} %bitcast.7) | data formatting | bytes 3932160
